TPU v7x, 32 devices: a whole 2x2x4 slice. The times are simulated.
32 devices in a mesh: rep: 4 (over y, core), shard: 8 (over z, x).
Axes of the slice: x: 2, y: 2, z: 4, core: 2. Of those that a mesh axis runs over, the one named last changes fastest.
Arguments:
- tokens: bfloat16 [8192, 1024], P(('rep', 'shard')), may hold values from -6 to 6
- cotangent: bfloat16 [8192, 1024], P(('rep', 'shard')), may hold values from -6 to 6
- qkv_weight: float32 [1024, 3072], P('shard'), may hold values from -0.1875 to 0.1875
- out_weight: float32 [1024, 1024], P('shard'), may hold values from -3 to 3
- up_weight: float32 [1024, 4096], P('shard'), may hold values from -0.1875 to 0.1875
- down_weight: float32 [4096, 1024], P('shard'), may hold values from -0.09375 to 0.09375
- gain_attn: float32 [1024], P('shard'), may hold values from 0.5 to 1.5
- gain_ffn: float32 [1024], P('shard'), may hold values from 0.5 to 1.5
- parents: int32 [4, 16], P('rep'), may hold values from 0 to 11, as said below
- slot_ids: int32 [64], P('rep'), may hold values from 0 to 15, as said below
Outputs:
- layer_out: bfloat16 [8192, 1024], P(('rep', 'shard'))
- input_grad: float32 [8192, 1024], P(('rep', 'shard'))
- qkv_grad: float32 [1024, 3072], P('shard')
- out_grad: float32 [1024, 1024], P('shard')
- up_grad: float32 [1024, 4096], P('shard')
- down_grad: float32 [4096, 1024], P('shard')
- attn_gain_grad: float32 [1024], P('shard')
- ffn_gain_grad: float32 [1024], P('shard')
Inputs may be any that keep to these rules, and one draw needn't show every extreme that they name: parents[t, 0] = 0; segment s of the trunk (1 <= s < 10) has parent s - 1; the 2 branch segments 10 .. 11 have parent 10 - 1; every later segment is a leaf whose parent is one of the branches, the last segment's parent being the last branch. `slot_ids`: each aligned block of 16 slots (one group) holds each number 0 .. 15 exactly once.
All inputs are finite; a program needn't handle non-finite values.
Results may differ from a plain program's by a relative error of at most 0.019.
Values may be sent and summed in bfloat16 or wider, within the bound.
A program may use at most 384 MiB of HBM per device.

v0:
```python
import jax
import jax.numpy as jnp
from jax import lax
from jax.sharding import PartitionSpec as P

HEADS = 16
HEAD = 64


masked_score = -1e30


def block_size():
    return 512


def normalize(values):
    average = jnp.mean(values, axis=-1, keepdims=True)
    centered = values - average
    variance = jnp.mean(centered * centered, axis=-1, keepdims=True)
    inv_std = lax.rsqrt(variance + 1e-05)
    return (centered * inv_std, inv_std)


def gelu_exact(values):
    return 0.5 * values * (1.0 + lax.erf(values * 0.7071067811865476))


def gelu_slope(values):
    return (
        0.5 * (1.0 + lax.erf(values * 0.7071067811865476))
        + values * jnp.exp(-0.5 * values * values) * 0.3989422804014327
    )


def norm_back(grad_normed, normed, inv_std):
    first_mean = jnp.mean(grad_normed, axis=-1, keepdims=True)
    second_mean = jnp.mean(grad_normed * normed, axis=-1, keepdims=True)
    return inv_std * (grad_normed - first_mean - normed * second_mean)


def times_t(left_side, right_side):
    return lax.dot_general(
        left_side, right_side, (((1,), (1,)), ((), ())), preferred_element_type=jnp.float32
    )


def t_times(left_side, right_side):
    return lax.dot_general(
        left_side, right_side, (((0,), (0,)), ((), ())), preferred_element_type=jnp.float32
    )


def exact_dot(left_side, right_side):
    return jnp.dot(
        left_side, right_side, precision=lax.Precision.HIGHEST, preferred_element_type=jnp.float32
    )


def slot_table(group_ids, parents):
    tree_segs = parents.shape[1]
    group_segs = group_ids.shape[0]
    seg_range = jnp.arange(tree_segs, dtype=jnp.int32)
    walker = seg_range[None, :]
    reached = walker[:, :, None] == seg_range[None, None, :]

    def climb(step_index, carried):
        walker_now, reached_now = carried
        walker_now = jnp.sum(
            jnp.where(walker_now[:, :, None] == seg_range[None, None, :], parents[:, None, :], 0),
            axis=2,
        )
        return (walker_now, reached_now | (walker_now[:, :, None] == seg_range[None, None, :]))

    walker, reached = lax.fori_loop(0, tree_segs, climb, (walker, reached))
    anc_flat = reached.reshape(group_segs, tree_segs).astype(jnp.float32)
    id_picks = (group_ids[:, None] == jnp.arange(group_segs, dtype=jnp.int32)[None, :]).astype(
        jnp.float32
    )
    seg_rows = exact_dot(id_picks, anc_flat)
    local_pick = ((group_ids % tree_segs)[:, None] == seg_range[None, :]).astype(jnp.float32)
    tree_of = group_ids // tree_segs
    same_tree = (tree_of[:, None] == tree_of[None, :]).astype(jnp.float32)
    return (
        lax.dot_general(
            seg_rows,
            local_pick,
            (((1,), (1,)), ((), ())),
            precision=lax.Precision.HIGHEST,
            preferred_element_type=jnp.float32,
        )
        * same_tree
    )


def visible_mask(allowed, seg_len, query_start, query_rows, key_start, key_rows):
    group_segs = allowed.shape[0]
    query_index = query_start + jnp.arange(query_rows, dtype=jnp.int32)
    key_index = key_start + jnp.arange(key_rows, dtype=jnp.int32)
    query_slot = query_index // seg_len
    key_slot = key_index // seg_len
    seg_range = jnp.arange(group_segs, dtype=jnp.int32)
    query_pick = (query_slot[:, None] == seg_range[None, :]).astype(jnp.float32)
    key_pick = (key_slot[:, None] == seg_range[None, :]).astype(jnp.float32)
    linked = (
        lax.dot_general(
            exact_dot(query_pick, allowed),
            key_pick,
            (((1,), (1,)), ((), ())),
            precision=lax.Precision.HIGHEST,
            preferred_element_type=jnp.float32,
        )
        > 0.5
    )
    return linked & (
        (query_slot[:, None] != key_slot[None, :]) | (key_index[None, :] <= query_index[:, None])
    )


def pair_terms(query_part, grad_part, stat_part, delta_part, key_part, value_part, visible):
    scores = (
        jnp.einsum("qhd,khd->qhk", query_part, key_part, preferred_element_type=jnp.float32) * 0.125
    )
    scores = jnp.where(visible[:, None, :], scores, masked_score)
    probs_full = jnp.exp(scores - stat_part[:, :, None])
    grad_probs = jnp.einsum(
        "qhd,khd->qhk", grad_part, value_part, preferred_element_type=jnp.float32
    )
    grad_scores = (probs_full * (grad_probs - delta_part[:, :, None])).astype(jnp.bfloat16)
    grad_query = None
    grad_key = None
    grad_value = None
    grad_query = (
        jnp.einsum("qhk,khd->qhd", grad_scores, key_part, preferred_element_type=jnp.float32)
        * 0.125
    )
    grad_key = (
        jnp.einsum("qhk,qhd->khd", grad_scores, query_part, preferred_element_type=jnp.float32)
        * 0.125
    )
    grad_value = jnp.einsum(
        "qhk,qhd->khd",
        probs_full.astype(jnp.bfloat16),
        grad_part,
        preferred_element_type=jnp.float32,
    )
    return (grad_query, grad_key, grad_value)


def shards(
    tokens,
    cotangent,
    qkv_weight,
    out_weight,
    up_weight,
    down_weight,
    gain_attn,
    gain_ffn,
    parents,
    slot_ids,
):
    local_rows = tokens.shape[0]
    model_width = tokens.shape[1]
    shard_count = lax.axis_size("shard")
    my_start = lax.axis_index("shard") * local_rows
    seg_len = local_rows * shard_count // slot_ids.shape[0]
    allowed = slot_table(slot_ids, parents)
    qkv_full, out_full, attn_gain = (
        lax.all_gather(qkv_weight.astype(jnp.bfloat16), "shard", axis=0, tiled=True),
        lax.all_gather(out_weight.astype(jnp.bfloat16), "shard", axis=0, tiled=True),
        lax.all_gather(gain_attn.astype(jnp.bfloat16), "shard", axis=0, tiled=True),
    )
    inputs = tokens.astype(jnp.float32)
    normed_one, inv_one = normalize(inputs)
    entered = (normed_one * attn_gain.astype(jnp.float32)).astype(jnp.bfloat16)
    qkv_all = jnp.dot(entered, qkv_full, preferred_element_type=jnp.float32).astype(jnp.bfloat16)
    queries = qkv_all[:, :model_width]
    keys_local = qkv_all[:, model_width : 2 * model_width]
    values_local = qkv_all[:, 2 * model_width :]
    query_heads = queries.reshape(local_rows, HEADS, HEAD)
    start_state = (
        jnp.full((local_rows, HEADS), masked_score, jnp.float32),
        jnp.zeros((local_rows, HEADS), jnp.float32),
        jnp.zeros((local_rows, HEADS, HEAD), jnp.float32),
    )
    carried = start_state
    key_piece = lax.all_gather(keys_local, "shard", axis=0, tiled=True)
    value_piece = lax.all_gather(values_local, "shard", axis=0, tiled=True)
    piece_rows = key_piece.shape[0]
    block_rows = block_size()
    count_blocks = piece_rows // block_rows
    key_blocks = key_piece.reshape(count_blocks, block_rows, HEADS, HEAD)
    value_blocks = value_piece.reshape(count_blocks, block_rows, HEADS, HEAD)

    def attend_block(running, blocks):
        key_block, value_block, block_index = blocks
        run_max, run_sum, run_acc = running
        visible = visible_mask(
            allowed, seg_len, my_start, local_rows, block_index * block_rows, block_rows
        )
        scores = (
            jnp.einsum("qhd,khd->qhk", query_heads, key_block, preferred_element_type=jnp.float32)
            * 0.125
        )
        scores = jnp.where(visible[:, None, :], scores, masked_score)
        new_max = jnp.maximum(run_max, jnp.max(scores, axis=2))
        rescale = jnp.exp(run_max - new_max)
        exp_scores = jnp.exp(scores - new_max[:, :, None])
        run_sum = run_sum * rescale + jnp.sum(exp_scores, axis=2)
        run_acc = run_acc * rescale[:, :, None] + jnp.einsum(
            "qhk,khd->qhd",
            exp_scores.astype(jnp.bfloat16),
            value_block,
            preferred_element_type=jnp.float32,
        )
        return ((new_max, run_sum, run_acc), None)

    carried, unused = lax.scan(
        attend_block, carried, (key_blocks, value_blocks, jnp.arange(count_blocks, dtype=jnp.int32))
    )
    run_max, run_sum, run_acc = carried
    attn_exact = run_acc / run_sum[:, :, None]
    log_sum = run_max + jnp.log(run_sum)
    attended = attn_exact.reshape(local_rows, model_width).astype(jnp.bfloat16)
    hidden = inputs + jnp.dot(attended, out_full, preferred_element_type=jnp.float32)
    up_full, down_full, ffn_gain = (
        lax.all_gather(up_weight.astype(jnp.bfloat16), "shard", axis=0, tiled=True),
        lax.all_gather(down_weight.astype(jnp.bfloat16), "shard", axis=0, tiled=True),
        lax.all_gather(gain_ffn.astype(jnp.bfloat16), "shard", axis=0, tiled=True),
    )
    normed_two, inv_two = normalize(hidden)
    second = (normed_two * ffn_gain.astype(jnp.float32)).astype(jnp.bfloat16)
    pre_act = jnp.dot(second, up_full, preferred_element_type=jnp.float32)
    active = gelu_exact(pre_act).astype(jnp.bfloat16)
    output = (hidden + jnp.dot(active, down_full, preferred_element_type=jnp.float32)).astype(
        jnp.bfloat16
    )
    up_full, down_full, ffn_gain = (
        lax.all_gather(up_weight.astype(jnp.bfloat16), "shard", axis=0, tiled=True),
        lax.all_gather(down_weight.astype(jnp.bfloat16), "shard", axis=0, tiled=True),
        lax.all_gather(gain_ffn.astype(jnp.bfloat16), "shard", axis=0, tiled=True),
    )
    qkv_full, out_full, attn_gain = (
        lax.all_gather(qkv_weight.astype(jnp.bfloat16), "shard", axis=0, tiled=True),
        lax.all_gather(out_weight.astype(jnp.bfloat16), "shard", axis=0, tiled=True),
        lax.all_gather(gain_attn.astype(jnp.bfloat16), "shard", axis=0, tiled=True),
    )
    grad_down = t_times(active, cotangent)
    grad_active = times_t(cotangent, down_full).astype(jnp.bfloat16)
    grad_pre = (grad_active.astype(jnp.float32) * gelu_slope(pre_act)).astype(jnp.bfloat16)
    grad_up = t_times(second, grad_pre)
    grad_second = times_t(grad_pre, up_full)
    grad_gain_ffn = jnp.sum(grad_second * normed_two, axis=0)
    grad_hidden = cotangent.astype(jnp.float32) + norm_back(
        grad_second * ffn_gain.astype(jnp.float32), normed_two, inv_two
    )
    grad_y = grad_hidden.astype(jnp.bfloat16)
    grad_out = t_times(attended, grad_y)
    grad_attn = times_t(grad_y, out_full).astype(jnp.bfloat16)
    grad_heads = grad_attn.reshape(local_rows, HEADS, HEAD)
    row_delta = jnp.sum(grad_heads.astype(jnp.float32) * attn_exact, axis=2)
    start_back = (
        jnp.zeros((local_rows, HEADS, HEAD), jnp.float32),
        jnp.zeros((local_rows * shard_count, 2 * model_width), jnp.float32),
    )
    carried = start_back
    key_piece = lax.all_gather(keys_local, "shard", axis=0, tiled=True)
    value_piece = lax.all_gather(values_local, "shard", axis=0, tiled=True)
    piece_rows = key_piece.shape[0]
    back_block_rows = block_size()
    count_blocks = piece_rows // back_block_rows
    key_blocks = key_piece.reshape(count_blocks, back_block_rows, HEADS, HEAD)
    value_blocks = value_piece.reshape(count_blocks, back_block_rows, HEADS, HEAD)

    def back_block(running, blocks):
        grad_query, key_terms = running
        key_block, value_block, block_index = blocks
        block_start = block_index * back_block_rows
        visible = visible_mask(allowed, seg_len, my_start, local_rows, block_start, back_block_rows)
        part_query, part_key, part_value = pair_terms(
            query_heads, grad_heads, log_sum, row_delta, key_block, value_block, visible
        )
        joined = jnp.concatenate(
            (
                part_key.reshape(back_block_rows, model_width),
                part_value.reshape(back_block_rows, model_width),
            ),
            axis=1,
        )
        key_terms = lax.dynamic_update_slice_in_dim(key_terms, joined, block_start, 0)
        return ((grad_query + part_query, key_terms), None)

    carried, unused = lax.scan(
        back_block, carried, (key_blocks, value_blocks, jnp.arange(count_blocks, dtype=jnp.int32))
    )
    grad_query, key_terms = carried
    key_grads = lax.psum_scatter(key_terms, "shard", scatter_dimension=0, tiled=True)
    grad_qkv = jnp.concatenate(
        (grad_query.reshape(local_rows, model_width), key_grads), axis=1
    ).astype(jnp.bfloat16)
    grad_qkv_weight = t_times(entered, grad_qkv)
    grad_entered = times_t(grad_qkv, qkv_full)
    grad_gain_attn = jnp.sum(grad_entered * normed_one, axis=0)
    input_grad = grad_hidden + norm_back(
        grad_entered * attn_gain.astype(jnp.float32), normed_one, inv_one
    )
    group_sums = (
        lax.psum_scatter(grad_qkv_weight, "shard", scatter_dimension=0, tiled=True),
        lax.psum_scatter(grad_out, "shard", scatter_dimension=0, tiled=True),
        lax.psum_scatter(grad_up, "shard", scatter_dimension=0, tiled=True),
        lax.psum_scatter(grad_down, "shard", scatter_dimension=0, tiled=True),
        lax.psum_scatter(grad_gain_attn, "shard", scatter_dimension=0, tiled=True),
        lax.psum_scatter(grad_gain_ffn, "shard", scatter_dimension=0, tiled=True),
    )
    totals = (
        lax.psum(group_sums[0].astype(jnp.bfloat16), "rep").astype(jnp.float32),
        lax.psum(group_sums[1].astype(jnp.bfloat16), "rep").astype(jnp.float32),
        lax.psum(group_sums[2].astype(jnp.bfloat16), "rep").astype(jnp.float32),
        lax.psum(group_sums[3].astype(jnp.bfloat16), "rep").astype(jnp.float32),
        lax.psum(group_sums[4].astype(jnp.bfloat16), "rep").astype(jnp.float32),
        lax.psum(group_sums[5].astype(jnp.bfloat16), "rep").astype(jnp.float32),
    )
    return (output, input_grad, totals[0], totals[1], totals[2], totals[3], totals[4], totals[5])


def solution(mesh):
    in_specs = (
        P(("rep", "shard"), None),
        P(("rep", "shard"), None),
        P("shard", None),
        P("shard", None),
        P("shard", None),
        P("shard", None),
        P("shard"),
        P("shard"),
        P("rep", None),
        P("rep"),
    )
    out_specs = (
        P(("rep", "shard"), None),
        P(("rep", "shard"), None),
        P("shard", None),
        P("shard", None),
        P("shard", None),
        P("shard", None),
        P("shard"),
        P("shard"),
    )
    return jax.shard_map(shards, mesh=mesh, in_specs=in_specs, out_specs=out_specs, check_vma=False)
```

profile of v0, /device:TPU:0, one launch (start us, length us, event | category | flops | bytes accessed | tf_op | source)
XLA Modules:
  0.0 1902.8 jit_solution(9166915411837722068)
XLA Ops:
  10.4 22.3 %all-gather = bf16[8,1,128]{2,1,0:T(2,128)(2,1)S(1)} all-gather(bf16[1,1,128]{2,1,0:T(2,128)(2,1)S(1)} %convert_bitcast_fusion.1), channel_id=1, replica_groups=mesh['rep'=4,'shard'=8] {'shard'}, dimensions={0}, use_global_device_ids=true | all-gather | bytes 2304 | tf_op jit(solution)/shard_map/all_gather | solution.py:171
  35.2 77.3 %all-gather.9.cloned.1.call-done = bf16[1024,3072]{1,0:T(8,128)(2,1)} async-done(((bf16[128,3072]{1,0:T(8,128)(2,1)}), bf16[1024,3072]{1,0:T(8,128)(2,1)}) %all-gather.9.cloned.1.call-update) | async-done | bytes 6291472 | tf_op jit(solution)/shard_map/all_gather | solution.py:169
  112.5 4.7 convolution_convert_fusion.1
  130.2 17.8 all-gather.1
  148.7 41.5 %all-gather.11.cloned.1.call-done = bf16[2048,1024]{1,0:T(8,128)(2,1)} async-done(((bf16[256,1024]{1,0:T(8,128)(2,1)}), bf16[2048,1024]{1,0:T(8,128)(2,1)}) %all-gather.11.cloned.1.call-update) | async-done | bytes 4194320 | tf_op jit(solution)/shard_map/all_gather | solution.py:187
  190.2 11.8 reshape.403
  202.0 9.8 copy.55
  211.8 52.8 %all-gather.13.cloned.1.call-done = bf16[2048,1024]{1,0:T(8,128)(2,1)} async-done(((bf16[256,1024]{1,0:T(8,128)(2,1)}), bf16[2048,1024]{1,0:T(8,128)(2,1)}) %all-gather.13.cloned.1.call-update) | async-done | bytes 4194320 | tf_op jit(solution)/shard_map/all_gather | solution.py:188
  264.6 11.7 reshape.404
  276.3 9.8 copy.56
  286.1 45.5 %while.49 = (s32[]{:T(128)}, f32[256,16]{0,1:T(8,128)S(1)}, f32[256,16]{0,1:T(8,128)S(1)}, f32[256,16,64]{0,2,1:T(8,128)}, s32[]{:T(128)}, /*index=5*/f32[16,16]...) while((s32[]{:T(128)}, f32[256,16]{0,1:T(8,128)S(1)}, ...), condition=%wide.region_8.9_spmd.clone, body=%wide.region_5.8_spmd.clone.sunk | while | flops 587378688 | bytes 39368944 | solution.py:218
  336.6 104.2 %all-gather.17.cloned.1.call-done = bf16[1024,4096]{1,0:T(8,128)(2,1)} async-done(((bf16[128,4096]{1,0:T(8,128)(2,1)}), bf16[1024,4096]{1,0:T(8,128)(2,1)}) %all-gather.17.cloned.1.call-update) | async-done | bytes 8388624 | tf_op jit(solution)/shard_map/all_gather | solution.py:227
  440.8 8.3 multiply_convert_fusion
  449.0 117.4 %all-gather.19.cloned.1.call-done = bf16[4096,1024]{1,0:T(8,128)(2,1)} async-done(((bf16[512,1024]{1,0:T(8,128)(2,1)}), bf16[4096,1024]{1,0:T(8,128)(2,1)}) %all-gather.19.cloned.1.call-update) | async-done | bytes 8388624 | tf_op jit(solution)/shard_map/all_gather | solution.py:228
  566.5 6.9 fusion.66
  582.9 7.8 broadcast_in_dim.74
  590.8 70.9 %while.50 = (s32[]{:T(128)}, f32[256,16,64]{0,2,1:T(8,128)S(1)}, f32[2048,2048]{0,1:T(8,128)}, bf16[4,512,16,64]{1,3,2,0:T(8,128)(2,1)}, s32[]{:T(128)}, /*index...) while((s32[]{:T(128)}, f32[256,16,64]{0,2,1:T(8,128)S(1)}, ...), condition=%wide.region_15.16_spmd.clone, body=%wide.region_14.15_spmd.clone.sunk | while | flops 1392140288 | bytes 60520720 | solution.py:293
  598.2 4.5 fusion.189
  615.9 4.5 fusion.189
  666.7 10.3 fusion.99
  678.0 9.7 fusion.103
  687.9 254.8 %reduce-scatter.6.cloned.1.call-done = f32[256,2048]{0,1:T(8,128)} async-done(((f32[2048,2048]{0,1:T(8,128)}), f32[256,2048]{0,1:T(8,128)}) %reduce-scatter.6.cloned.1.call-update) | async-done | bytes 2097168 | tf_op jit(solution)/shard_map/reduce_scatter | solution.py:297
  944.4 6.5 fusion.85
  952.8 81.0 %reduce-scatter.10.cloned.1.call-done = f32[128,1024]{1,0:T(8,128)} async-done(((f32[1024,1024]{1,0:T(8,128)}), f32[128,1024]{1,0:T(8,128)}) %reduce-scatter.10.cloned.1.call-update) | async-done | bytes 524304 | tf_op jit(solution)/shard_map/reduce_scatter | solution.py:309
  1035.5 284.5 %reduce-scatter.12.cloned.1.call-done = f32[128,4096]{1,0:T(8,128)} async-done(((f32[1024,4096]{1,0:T(8,128)}), f32[128,4096]{1,0:T(8,128)}) %reduce-scatter.12.cloned.1.call-update) | async-done | bytes 2097168 | tf_op jit(solution)/shard_map/reduce_scatter | solution.py:310
  1322.7 283.2 %reduce-scatter.14.cloned.1.call-done = f32[512,1024]{1,0:T(8,128)} async-done(((f32[4096,1024]{1,0:T(8,128)}), f32[512,1024]{1,0:T(8,128)}) %reduce-scatter.14.cloned.1.call-update) | async-done | bytes 2097168 | tf_op jit(solution)/shard_map/reduce_scatter | solution.py:311
  1608.6 207.3 %reduce-scatter.8.cloned.1.call-done = f32[128,3072]{1,0:T(8,128)} async-done(((f32[1024,3072]{1,0:T(8,128)}), f32[128,3072]{1,0:T(8,128)}) %reduce-scatter.8.cloned.1.call-update) | async-done | bytes 1572880 | tf_op jit(solution)/shard_map/reduce_scatter | solution.py:308
  1818.4 7.2 fusion.71
  1825.6 5.1 fusion.83
  1830.7 19.8 %all-reduce.2 = (bf16[1024]{0:T(1024)(128)(2,1)S(1)}, bf16[1024]{0:T(1024)(128)(2,1)S(1)}) all-reduce(f32[1024]{0:T(1024)S(1)} %get-tuple-element.547, f32[1024]{0:T(1024)S(1)} %get-tuple-element.545), channel_id=7, replica_groups=mesh['rep'=4,'shard'=8] {'shard'}, use_global_device_ids=true, to_apply=%region_28.29.clone | all-reduce | flops 2048 | bytes 12288
  1850.6 5.6 all-reduce.3
  1858.7 28.5 %all-reduce.7.cloned.1.call-done = (bf16[128,3072]{1,0:T(8,128)(2,1)}, bf16[128,1024]{1,0:T(8,128)(2,1)}, bf16[128,4096]{1,0:T(8,128)(2,1)}, bf16[512,1024]{1,0:T(8,128)(2,1)}) async-done(((bf16[128,3072]{1,0:T(8,128)(2,1)}, bf16[128,1024]{1,0:T(8,128)(2,1)}, bf16[128,4096]{1,0:T(8,128)(2,1)}, bf16[512,1024]{1,0:T(8,128)(2,1)}), (bf16[128,3072]{1,0:T(8,128)(2,1)}, bf16[128,1024]{1,0:T(8,128)(2,1)}, ...) | async-done | bytes 3145744 | tf_op jit(solution)/shard_map/psum | solution.py:316
  (294 shorter events, 168.9 us)
Async XLA Ops:
  7.2 105.4 %copy-start.2 = (bf16[256,1024]{1,0:T(8,128)(2,1)S(1)}, bf16[256,1024]{1,0:T(8,128)(2,1)}, u32[]{:S(2)}) copy-start(bf16[256,1024]{1,0:T(8,128)(2,1)} %param.16) | copy-start | bytes 1572868
  7.2 105.4 %all-gather.9.cloned.1.call-start = ((), (), s32[]{:S(2)}) async-start(), calls=%async_computation.5 | async-start | bytes 7077888 | tf_op jit(solution)/shard_map/all_gather | solution.py:169
  9.7 180.5 %all-gather.11.cloned.1.call-start = ((), (), s32[]{:S(2)}) async-start(), calls=%async_computation.6 | async-start | bytes 4718592 | tf_op jit(solution)/shard_map/all_gather | solution.py:187
  32.7 84.6 %copy-start.15 = (f32[8,1,128]{2,1,0:T(1,128)}, f32[8,1,128]{2,1,0:T(1,128)S(1)}, u32[]{:S(2)}) copy-start(f32[8,1,128]{2,1,0:T(1,128)S(1)} %convert_element_type.178) | copy-start | bytes 12292
  33.9 83.4 %copy-start.17 = (f32[256]{0:T(256)}, f32[256]{0:T(256)S(1)}, u32[]{:S(2)}) copy-start(f32[256]{0:T(256)S(1)} %broadcast_multiply_fusion.5) | copy-start | bytes 3076
  35.2 82.0 %copy-start.19 = (f32[256]{0:T(256)}, f32[256]{0:T(256)S(1)}, u32[]{:S(2)}) copy-start(f32[256]{0:T(256)S(1)} %add_rsqrt_fusion.1) | copy-start | bytes 3076
  118.4 146.2 %all-gather.13.cloned.1.call-start = ((), (), s32[]{:S(2)}) async-start(), calls=%async_computation.7 | async-start | bytes 4718592 | tf_op jit(solution)/shard_map/all_gather | solution.py:188
  119.1 214.6 %all-gather.15.cloned.1.call-start = ((), (), s32[]{:S(2)}) async-start(), calls=%async_computation.8 | async-start | bytes 2359296 | tf_op jit(solution)/shard_map/all_gather | solution.py:170
  120.0 5.9 copy-start.22
  120.0 10.2 copy-start.23
  120.0 28.1 %copy-start.24 = (s32[16]{0:T(128)S(1)}, s32[16]{0:T(128)}, u32[]{:S(2)}) copy-start(s32[16]{0:T(128)} %param.25) | copy-start | bytes 196
  120.0 320.8 %all-gather.17.cloned.1.call-start = ((), (), s32[]{:S(2)}) async-start(), calls=%async_computation.9 | async-start | bytes 9437184 | tf_op jit(solution)/shard_map/all_gather | solution.py:227
  122.8 443.7 %all-gather.19.cloned.1.call-start = ((), (), s32[]{:S(2)}) async-start(), calls=%async_computation.10 | async-start | bytes 9437184 | tf_op jit(solution)/shard_map/all_gather | solution.py:228
  125.7 817.0 %reduce-scatter.6.cloned.1.call-start = ((), (), s32[]{:S(2)}) async-start(), calls=%async_computation.11 | async-start | bytes 18874368 | tf_op jit(solution)/shard_map/reduce_scatter | solution.py:297
  566.5 7.2 copy-start.21
  573.6 2.7 copy-start.9
  573.6 2.7 copy-start.10
  573.6 4.1 copy-start.3
  611.2 2.6 copy-start.12
  628.7 2.6 copy-start.12
  661.7 372.1 %reduce-scatter.10.cloned.1.call-start = ((), (), s32[]{:S(2)}) async-start(), calls=%async_computation.13 | async-start | bytes 4718592 | tf_op jit(solution)/shard_map/reduce_scatter | solution.py:309
  666.6 653.3 %reduce-scatter.12.cloned.1.call-start = ((), (), s32[]{:S(2)}) async-start(), calls=%async_computation.14 | async-start | bytes 18874368 | tf_op jit(solution)/shard_map/reduce_scatter | solution.py:310
  677.0 928.9 %reduce-scatter.14.cloned.1.call-start = ((), (), s32[]{:S(2)}) async-start(), calls=%async_computation.15 | async-start | bytes 18874368 | tf_op jit(solution)/shard_map/reduce_scatter | solution.py:311
  687.7 256.6 %copy-start.16 = (f32[8,1,128]{2,1,0:T(1,128)S(1)}, f32[8,1,128]{2,1,0:T(1,128)}, u32[]{:S(2)}) copy-start(f32[8,1,128]{2,1,0:T(1,128)} %copy-done.15) | copy-start | bytes 12292
  687.7 256.6 %copy-start.18 = (f32[256]{0:T(256)S(1)}, f32[256]{0:T(256)}, u32[]{:S(2)}) copy-start(f32[256]{0:T(256)} %copy-done.17) | copy-start | bytes 3076
  687.7 256.6 %copy-start.20 = (f32[256]{0:T(256)S(1)}, f32[256]{0:T(256)}, u32[]{:S(2)}) copy-start(f32[256]{0:T(256)} %copy-done.19) | copy-start | bytes 3076
  687.8 1128.1 %reduce-scatter.8.cloned.1.call-start = ((), (), s32[]{:S(2)}) async-start(), calls=%async_computation.12 | async-start | bytes 14155776 | tf_op jit(solution)/shard_map/reduce_scatter | solution.py:308
  944.3 6.5 copy-start.5
  950.9 936.2 %all-reduce.7.cloned.1.call-start = ((), (), s32[]{:S(2)}) async-start(), calls=%async_computation.16 | async-start | bytes 6291456 | tf_op jit(solution)/shard_map/psum | solution.py:316
  1818.4 7.2 copy-start.6
  1825.6 31.7 %copy-start.1 = (f32[256,1024]{1,0:T(8,128)S(1)}, f32[256,1024]{1,0:T(8,128)}, u32[]{:S(2)}) copy-start(f32[256,1024]{1,0:T(8,128)} %copy-done) | copy-start | bytes 3145732
  1887.1 7.1 copy-start.13
  (15 other events, 21.7 us)
Sparse Core Ops, SparseCore 0:
  10.8 101.7 all-gather.8
  118.5 71.6 all-gather.10
  192.9 71.6 all-gather.12
  267.2 47.5 all-gather.14
  317.3 123.4 all-gather.16
  443.3 123.1 all-gather.18
  661.8 280.7 reduce-scatter.5
  946.7 86.9 reduce-scatter.9
  1037.5 282.3 reduce-scatter.11
  1324.1 281.7 reduce-scatter.13
  1609.4 206.4 reduce-scatter.7
  1818.9 68.1 all-reduce.6
where the time goes:
time: 1910 us; the launch traced here: 1900 us
  waiting for transfers between devices  1530 us (80%)
  matrix products  152 us (8%)
  local copies, waits for them, and re-layouts  69.3 us (4%)
  blocking collectives  65.5 us (3%)
  other arithmetic  60.3 us (3%)
    reduce_scatter x1, waiting for transfers between devices, shards(): lax.psum_scatter(grad_up, 'shard', scatter_dimension=0, tiled=True)  284 us
    reduce_scatter x1, waiting for transfers between devices, shards(): lax.psum_scatter(grad_down, 'shard', scatter_dimension=0, tiled=True)  283 us
    reduce_scatter x1, waiting for transfers between devices, shards(): lax.psum_scatter(key_terms, 'shard', scatter_dimension=0, tiled=True)  255 us
    reduce_scatter x1, waiting for transfers between devices, shards(): lax.psum_scatter(grad_qkv_weight, 'shard', scatter_dimension=0, tiled=True)  207 us
    all_gather x1, waiting for transfers between devices, shards(): lax.all_gather(down_weight.astype(jnp.bfloat16), 'shard', axis=0, tiled=T...  117 us
    all_gather x1, waiting for transfers between devices, shards(): lax.all_gather(up_weight.astype(jnp.bfloat16), 'shard', axis=0, tiled=True)  104 us
    reduce_scatter x1, waiting for transfers between devices, shards(): lax.psum_scatter(grad_out, 'shard', scatter_dimension=0, tiled=True)  81 us
    all_gather x1, waiting for transfers between devices, shards(): lax.all_gather(qkv_weight.astype(jnp.bfloat16), 'shard', axis=0, tiled=True)  77.3 us
  transfers between devices with their start and end apart: 12, of which 11 were waited for; matrix products, arithmetic and copies ran while one was open for 9% of the time, Pallas kernels for 0%

commit v1 on v0

--- a/solution.py
+++ b/solution.py
@@ -1,6 +1,8 @@
 import jax
 import jax.numpy as jnp
 from jax import lax
+from jax.experimental import pallas as pl
+from jax.experimental.pallas import tpu as pltpu
 from jax.sharding import PartitionSpec as P
 
 HEADS = 16
@@ -259,10 +261,7 @@
     grad_attn = times_t(grad_y, out_full).astype(jnp.bfloat16)
     grad_heads = grad_attn.reshape(local_rows, HEADS, HEAD)
     row_delta = jnp.sum(grad_heads.astype(jnp.float32) * attn_exact, axis=2)
-    start_back = (
-        jnp.zeros((local_rows, HEADS, HEAD), jnp.float32),
-        jnp.zeros((local_rows * shard_count, 2 * model_width), jnp.float32),
-    )
+    start_back = jnp.zeros((local_rows, HEADS, HEAD), jnp.float32)
     carried = start_back
     key_piece = lax.all_gather(keys_local, "shard", axis=0, tiled=True)
     value_piece = lax.all_gather(values_local, "shard", axis=0, tiled=True)
@@ -273,7 +272,7 @@
     value_blocks = value_piece.reshape(count_blocks, back_block_rows, HEADS, HEAD)
 
     def back_block(running, blocks):
-        grad_query, key_terms = running
+        grad_query = running
         key_block, value_block, block_index = blocks
         block_start = block_index * back_block_rows
         visible = visible_mask(allowed, seg_len, my_start, local_rows, block_start, back_block_rows)
@@ -287,13 +286,13 @@
             ),
             axis=1,
         )
-        key_terms = lax.dynamic_update_slice_in_dim(key_terms, joined, block_start, 0)
-        return ((grad_query + part_query, key_terms), None)
-
-    carried, unused = lax.scan(
+        return (grad_query + part_query, joined.astype(jnp.bfloat16))
+
+    carried, key_terms = lax.scan(
         back_block, carried, (key_blocks, value_blocks, jnp.arange(count_blocks, dtype=jnp.int32))
     )
-    grad_query, key_terms = carried
+    grad_query = carried
+    key_terms = key_terms.reshape(piece_rows, 2 * model_width)
     key_grads = lax.psum_scatter(key_terms, "shard", scatter_dimension=0, tiled=True)
     grad_qkv = jnp.concatenate(
         (grad_query.reshape(local_rows, model_width), key_grads), axis=1
@@ -305,10 +304,10 @@
         grad_entered * attn_gain.astype(jnp.float32), normed_one, inv_one
     )
     group_sums = (
-        lax.psum_scatter(grad_qkv_weight, "shard", scatter_dimension=0, tiled=True),
-        lax.psum_scatter(grad_out, "shard", scatter_dimension=0, tiled=True),
-        lax.psum_scatter(grad_up, "shard", scatter_dimension=0, tiled=True),
-        lax.psum_scatter(grad_down, "shard", scatter_dimension=0, tiled=True),
+        lax.psum_scatter(grad_qkv_weight.astype(jnp.bfloat16), "shard", scatter_dimension=0, tiled=True),
+        lax.psum_scatter(grad_out.astype(jnp.bfloat16), "shard", scatter_dimension=0, tiled=True),
+        lax.psum_scatter(grad_up.astype(jnp.bfloat16), "shard", scatter_dimension=0, tiled=True),
+        lax.psum_scatter(grad_down.astype(jnp.bfloat16), "shard", scatter_dimension=0, tiled=True),
         lax.psum_scatter(grad_gain_attn, "shard", scatter_dimension=0, tiled=True),
         lax.psum_scatter(grad_gain_ffn, "shard", scatter_dimension=0, tiled=True),
     )
@@ -321,6 +320,823 @@
         lax.psum(group_sums[5].astype(jnp.bfloat16), "rep").astype(jnp.float32),
     )
     return (output, input_grad, totals[0], totals[1], totals[2], totals[3], totals[4], totals[5])
+
+
+MESH = pl.DeviceIdType.MESH
+
+
+def ring_place(shard):
+    return (1 - shard % 2) * (shard // 2) + (shard % 2) * (7 - shard // 2)
+
+
+def ring_shard(place):
+    upper = place // 4
+    return (1 - upper) * 2 * place + upper * (15 - 2 * place)
+
+
+def remote(source, target, sent, got, device):
+    return pltpu.make_async_remote_copy(
+        src_ref=source,
+        dst_ref=target,
+        send_sem=sent,
+        recv_sem=got,
+        device_id=device,
+        device_id_type=MESH,
+    )
+
+
+def around(place, offset):
+    return ring_shard(lax.rem(place + offset + 8, 8))
+
+
+class Where:
+    def __init__(self):
+        self.rep = lax.axis_index("rep")
+        self.me = lax.axis_index("shard")
+        self.y = self.rep // 2
+        self.core = self.rep % 2
+        self.rep_y = (1 - self.y) * 2 + self.core
+        self.rep_core = self.y * 2 + 1 - self.core
+        self.rep_far = (1 - self.y) * 2 + 1 - self.core
+        self.place = ring_place(self.me)
+        self.right = around(self.place, 1)
+        self.left = around(self.place, -1)
+
+    def other(self, step):
+        return lax.rem(self.me + step, 8)
+
+    def back(self, step):
+        return lax.rem(self.me + 8 - step, 8)
+
+    def greet(self):
+        barrier = pltpu.get_barrier_semaphore()
+        for step in range(1, 8):
+            pl.semaphore_signal(
+                barrier, inc=1, device_id=(self.rep, self.other(step)), device_id_type=MESH
+            )
+        for rep in (self.rep_y, self.rep_core, self.rep_far):
+            pl.semaphore_signal(barrier, inc=1, device_id=(rep, self.me), device_id_type=MESH)
+        pl.semaphore_wait(barrier, 10)
+
+
+RING_UNITS = [(flow, step, piece) for step in range(3) for flow in range(2) for piece in range(3)]
+RING_UNITS = RING_UNITS + [(0, 3, 1), (1, 3, 2), (1, 3, 0)]
+
+
+def normed_rows(values):
+    average = jnp.mean(values, axis=-1, keepdims=True)
+    centered = values - average
+    variance = jnp.mean(centered * centered, axis=-1, keepdims=True)
+    inv_std = lax.rsqrt(variance + 1e-05)
+    return (centered * inv_std, inv_std)
+
+
+def gain_row(gains_ref, which):
+    return jnp.concatenate(
+        [gains_ref[s, which * 8 : which * 8 + 1, :] for s in range(8)], axis=1
+    ).astype(jnp.float32)
+
+
+def head_lanes(values, head):
+    lane = lax.broadcasted_iota(jnp.int32, values.shape, 1)
+    return jnp.where(lane // HEAD == head, values, jnp.zeros_like(values))
+
+
+KEY_ROWS = [256, 512, 768, 1024, 1280, 1536, 1536, 1536]
+
+
+def tile_masks(block, parents_ref):
+    key_row = lax.broadcasted_iota(jnp.int32, (256, 256), 0)
+    query_row = lax.broadcasted_iota(jnp.int32, (256, 256), 1)
+    own = key_row <= query_row
+    if block < 5:
+        return (own, None)
+    own = own & (key_row // 128 == query_row // 128)
+    if block == 5:
+        return (own, None)
+    parent = jnp.where(query_row < 128, parents_ref[2 * block], parents_ref[2 * block + 1])
+    return (own, parent == 10 + key_row // 128)
+
+
+def score_parts(block, keys_ref, queries, masks):
+    own_mask, branch_mask = masks
+    full = 256 * block if block < 5 else 1280
+    spans = [(0, full, None)] if full else []
+    if branch_mask is not None:
+        spans.append((1280, 256, branch_mask))
+    spans.append((256 * block, 256, own_mask))
+    parts = []
+    for first, rows, mask in spans:
+        scores = times_t(keys_ref[pl.ds(first, rows), :], queries)
+        if mask is not None:
+            scores = jnp.where(mask, scores, masked_score)
+        parts.append((first, rows, scores))
+    return parts
+
+
+def forward_kernel(
+    place_ref, ids_ref, parents_ref, tok_ref, wq_ref, gain_ref, out_ref, up_ref, down_ref,
+    att_ref, ent_ref, qkv_ref, mixed_ref, log_ref, gains_ref, slice_ref, out_all, up_all, down_all,
+    tok_all, qkv_slots, value_t, tree_rows, slot_rows,
+    small_s, small_r, tok_s, tok_r, ring_s, ring_r, y_s, y_r, core_s, core_r, mix_s, mix_r, local_s,
+):
+    at = Where()
+    rep, me = at.rep, at.me
+    at.greet()
+    ring_device = ((rep, at.right), (rep, at.left))
+
+    small = []
+    for step in range(1, 8):
+        to = at.other(step)
+        small.append(
+            remote(
+                gain_ref, gains_ref.at[me], small_s.at[0, step], small_r.at[0, step], (rep, to)
+            )
+        )
+        small.append(
+            remote(
+                wq_ref.at[to],
+                slice_ref.at[me],
+                small_s.at[1, step],
+                small_r.at[1, step],
+                (rep, to),
+            )
+        )
+
+    def token_copy(flow, step, half):
+        origin = around(at.place, step if flow else -step)
+        source = tok_ref if step == 0 else tok_all.at[origin]
+        rows = pl.ds(half * 128, 128)
+        return remote(
+            source.at[rows, :],
+            tok_all.at[origin, rows, :],
+            tok_s.at[flow, step, half],
+            tok_r.at[flow, step, half],
+            ring_device[flow],
+        )
+
+    def piece_rows(piece, origin, quarter):
+        whole = (out_all, up_all, down_all)[piece]
+        if piece < 2:
+            return whole.at[pl.ds(origin * 128 + quarter * 32, 32), :]
+        return whole.at[pl.ds(origin * 512 + quarter * 128, 128), :]
+
+    def ring_copy(unit):
+        flow, step, piece = unit
+        origin = around(at.place, step if flow else -step)
+        index = RING_UNITS.index(unit)
+        target = piece_rows(piece, origin, rep)
+        if step == 0:
+            source = (out_ref, up_ref, down_ref)[piece]
+            rows = 32 if piece < 2 else 128
+            source = source.at[pl.ds(rep * rows, rows), :]
+        else:
+            source = target
+        return remote(source, target, ring_s.at[index], ring_r.at[index], ring_device[flow])
+
+    def unit_origin(unit):
+        flow, step, _ = unit
+        return around(at.place, (step + 1) if flow else -(step + 1))
+
+    def share_y(unit):
+        index = RING_UNITS.index(unit)
+        block = piece_rows(unit[2], unit_origin(unit), rep)
+        return remote(block, block, y_s.at[index], y_r.at[index], (at.rep_y, me))
+
+    def share_core(unit, own):
+        index = RING_UNITS.index(unit)
+        block = piece_rows(unit[2], unit_origin(unit), rep if own else at.rep_y)
+        return remote(
+            block, block, core_s.at[own, index], core_r.at[own, index], (at.rep_core, me)
+        )
+
+    for copy in small:
+        copy.start()
+    for half in range(2):
+        for flow in range(2):
+            token_copy(flow, 0, half).start()
+    for unit in RING_UNITS:
+        if unit[1] == 0:
+            ring_copy(unit).start()
+    kept = [
+        pltpu.make_async_copy(out_ref, out_all.at[pl.ds(me * 128, 128), :], local_s.at[0]),
+        pltpu.make_async_copy(up_ref, up_all.at[pl.ds(me * 128, 128), :], local_s.at[1]),
+        pltpu.make_async_copy(down_ref, down_all.at[pl.ds(me * 512, 512), :], local_s.at[2]),
+    ]
+    for copy in kept:
+        copy.start()
+    gains_ref[me] = gain_ref[...]
+    slice_ref[me] = wq_ref[me]
+    for copy in small:
+        copy.wait_recv()
+    gain = gain_row(gains_ref, 0)
+
+    def enter(rows, origin):
+        normed, _ = normed_rows(rows.astype(jnp.float32))
+        entered = (normed * gain).astype(jnp.bfloat16)
+        ent_ref[origin] = entered
+        weights = slice_ref[...].reshape(1024, 384)
+        made = jnp.dot(entered, weights, preferred_element_type=jnp.float32).astype(jnp.bfloat16)
+        qkv_slots[2 * origin] = made[:128]
+        qkv_slots[2 * origin + 1] = made[128:]
+
+    enter(tok_ref[...], me)
+
+    for step in range(4):
+        halves = [(half, flow) for half in range(2) for flow in range(2)]
+        if step == 3:
+            halves = [(0, 0), (1, 1)]
+        for half, flow in halves:
+            token_copy(flow, step, half).wait_recv()
+            if step < 2 or (step == 2 and half == flow):
+                token_copy(flow, step + 1, half).start()
+        for unit in RING_UNITS:
+            if unit[1] == step:
+                ring_copy(unit).wait_recv()
+                after = (unit[0], step + 1, unit[2])
+                if after in RING_UNITS:
+                    ring_copy(after).start()
+                share_y(unit).start()
+                share_core(unit, 1).start()
+        for flow in range(2 if step < 3 else 1):
+            origin = around(at.place, (step + 1) if flow else -(step + 1))
+            enter(tok_all[origin], origin)
+
+    for seg in range(16):
+        rows = qkv_slots[place_ref[seg]]
+        qkv_ref[seg * 128 : seg * 128 + 128, :] = rows
+    for block in range(8):
+        rows = pl.ds(block * 256, 256)
+        value_t[:, block * 256 : block * 256 + 256] = qkv_ref[rows, 256:384].T
+
+    for block in range(8):
+        masks = tile_masks(block, parents_ref)
+        rows = pl.ds(block * 256, 256)
+
+        def one_head(head, unused):
+            queries = head_lanes(qkv_ref[rows, 0:128], head) * jnp.bfloat16(0.125)
+            parts = score_parts(block, qkv_ref.at[:, pl.ds(128, 128)], queries, masks)
+            top = None
+            for _, _, scores in parts:
+                part = jnp.max(scores, axis=0, keepdims=True)
+                top = part if top is None else jnp.maximum(top, part)
+            total = None
+            mixed = None
+            head_rows = pl.ds(pl.multiple_of(head * HEAD, HEAD), HEAD)
+            for first, count, scores in parts:
+                weights = jnp.exp(scores - top)
+                part = jnp.sum(weights, axis=0, keepdims=True)
+                total = part if total is None else total + part
+                term = jnp.dot(
+                    value_t[head_rows, pl.ds(first, count)],
+                    weights.astype(jnp.bfloat16),
+                    preferred_element_type=jnp.float32,
+                )
+                mixed = term if mixed is None else mixed + term
+            mixed_ref[head_rows, block * 256 : block * 256 + 256] = mixed / total
+            log_ref[pl.ds(pl.multiple_of(head * 8, 8), 8), block * 256 : block * 256 + 256] = (
+                jnp.broadcast_to(top + jnp.log(total), (8, 256))
+            )
+            return unused
+
+        lax.fori_loop(0, 2, one_head, 0)
+        tree = mixed_ref[:, block * 256 : block * 256 + 256].T.astype(jnp.bfloat16)
+        tree_rows[2 * block] = tree[:128]
+        tree_rows[2 * block + 1] = tree[128:]
+
+    for slot in range(16):
+        slot_rows[slot // 2, (slot % 2) * 128 : (slot % 2) * 128 + 128, :] = tree_rows[
+            ids_ref[slot]
+        ]
+
+    columns = pl.ds(pl.multiple_of(me * 128, 128), 128)
+    mix = []
+    for step in range(1, 8):
+        to = at.other(step)
+        mix.append(
+            remote(
+                slot_rows.at[to],
+                att_ref.at[:, columns],
+                mix_s.at[step],
+                mix_r.at[step],
+                (rep, to),
+            )
+        )
+    for copy in mix:
+        copy.start()
+    att_ref[:, columns] = slot_rows[me]
+
+    for unit in RING_UNITS:
+        share_y(unit).wait_recv()
+        share_core(unit, 0).start()
+    for copy in mix:
+        copy.wait()
+    for copy in kept:
+        copy.wait()
+    for unit in RING_UNITS:
+        share_core(unit, 1).wait()
+        share_core(unit, 0).wait()
+        share_y(unit).wait_send()
+        ring_copy(unit).wait_send()
+    for copy in small:
+        copy.wait_send()
+    for step in range(4):
+        for half in range(2):
+            for flow in range(2):
+                if step < 3 or half == flow:
+                    token_copy(flow, step, half).wait_send()
+
+
+def forward_part(places, slot_ids, parents, tokens, wq, gains, out_b, up_b, down_b):
+    smem = pl.BlockSpec(memory_space=pltpu.SMEM)
+    vmem = pl.BlockSpec(memory_space=pltpu.VMEM)
+    anywhere = pl.BlockSpec(memory_space=pl.ANY)
+    units = len(RING_UNITS)
+    dma = pltpu.SemaphoreType.DMA
+    return pl.pallas_call(
+        forward_kernel,
+        out_shape=[
+            jax.ShapeDtypeStruct((256, 1024), jnp.bfloat16),
+            jax.ShapeDtypeStruct((8, 256, 1024), jnp.bfloat16),
+            jax.ShapeDtypeStruct((2048, 384), jnp.bfloat16),
+            jax.ShapeDtypeStruct((128, 2048), jnp.float32),
+            jax.ShapeDtypeStruct((16, 2048), jnp.float32),
+            jax.ShapeDtypeStruct((8, 16, 128), jnp.bfloat16),
+            jax.ShapeDtypeStruct((8, 128, 384), jnp.bfloat16),
+            jax.ShapeDtypeStruct((1024, 1024), jnp.bfloat16),
+            jax.ShapeDtypeStruct((1024, 4096), jnp.bfloat16),
+            jax.ShapeDtypeStruct((4096, 1024), jnp.bfloat16),
+        ],
+        in_specs=[smem] * 3 + [vmem] * 3 + [anywhere] * 3,
+        out_specs=[vmem] * 7 + [anywhere] * 3,
+        scratch_shapes=[
+            pltpu.VMEM((8, 256, 1024), jnp.bfloat16),
+            pltpu.VMEM((16, 128, 384), jnp.bfloat16),
+            pltpu.VMEM((128, 2048), jnp.bfloat16),
+            pltpu.VMEM((16, 128, 128), jnp.bfloat16),
+            pltpu.VMEM((8, 256, 128), jnp.bfloat16),
+            dma((2, 8)), dma((2, 8)), dma((2, 4, 2)), dma((2, 4, 2)),
+            dma((units,)), dma((units,)), dma((units,)), dma((units,)),
+            dma((2, units)), dma((2, units)), dma((8,)), dma((8,)), dma((3,)),
+        ],
+        compiler_params=pltpu.CompilerParams(
+            collective_id=1, has_side_effects=True, vmem_limit_bytes=56 * 2**20
+        ),
+    )(places, slot_ids, parents, tokens, wq, gains, out_b, up_b, down_b)
+
+
+BLOCK_ORDER = [4, 3, -3, 2, -2, 1, -1, 0]
+
+
+def summed(*parts):
+    total = parts[0].astype(jnp.float32)
+    for part in parts[1:]:
+        total = total + part.astype(jnp.float32)
+    return total
+
+
+def backward_kernel(
+    place_ref, ids_ref, parents_ref, tok_ref, gh_ref, ga_ref, ent_ref, qkv_ref, mixed_ref, log_ref,
+    gains_ref, slice_ref, gfg_ref, out_ref, up_ref, down_ref,
+    in_ref, qkv_out, out_out, up_out, down_out, gain_out,
+    own_out, own_up, own_down, cr_out, cr_up, cr_down, yr_out, yr_up, yr_down, rr_out, rr_up, rr_down,
+    do_slots, do_tree, key_t, dq_t, dk, dv, gq_tree, gq_slots, gq_t, ge_recv,
+    qs_send, qs_recv, qs_core, qs_half, qs_y, gp, gp_recv, gp_rep,
+    do_s, do_r, load_s, core_s, core_r, y_s, y_r, ring_s, ring_r, fin_s, fin_r, ge_s, ge_r,
+    qs_s, qs_r, qr_s, qr_r, gp_s, gp_r, gr_s, gr_r,
+):
+    at = Where()
+    rep, me, y, core = at.rep, at.me, at.y, at.core
+    at.greet()
+    ring_device = ((rep, at.right), (rep, at.left))
+    whole = (out_ref, up_ref, down_ref)
+    own = (own_out, own_up, own_down)
+    from_core = (cr_out, cr_up, cr_down)
+    from_y = (yr_out, yr_up, yr_down)
+    from_ring = (rr_out, rr_up, rr_down)
+    result = (out_out, up_out, down_out)
+    order = [around(at.place, offset) for offset in BLOCK_ORDER]
+
+    grads = []
+    for step in range(1, 8):
+        to = at.other(step)
+        grads.append(
+            remote(
+                ga_ref.at[:, pl.ds(pl.multiple_of(to * 128, 128), 128)],
+                do_slots.at[me],
+                do_s.at[step],
+                do_r.at[step],
+                (rep, to),
+            )
+        )
+    for copy in grads:
+        copy.start()
+    loads = [
+        pltpu.make_async_copy(whole[i].at[:, :, core], own[i], load_s.at[i]) for i in range(3)
+    ]
+    for copy in loads:
+        copy.start()
+
+    def core_copy(index, piece):
+        block = order[index]
+        return remote(
+            whole[piece].at[block, :, 1 - core],
+            from_core[piece].at[block],
+            core_s.at[index, piece],
+            core_r.at[index, piece],
+            (at.rep_core, me),
+        )
+
+    def y_copy(index, piece):
+        block = order[index]
+        return remote(
+            own[piece].at[block, 1 - y],
+            from_y[piece].at[block],
+            y_s.at[index, piece],
+            y_r.at[index, piece],
+            (at.rep_y, me),
+        )
+
+    for index in range(8):
+        for piece in range(3):
+            core_copy(index, piece).start()
+    do_slots[me] = ga_ref[:, pl.ds(pl.multiple_of(me * 128, 128), 128)]
+    for copy in loads:
+        copy.wait()
+    for index in range(8):
+        block = order[index]
+        for piece in range(3):
+            core_copy(index, piece).wait_recv()
+            own[piece][block, 1 - y] = summed(
+                own[piece][block, 1 - y], from_core[piece][block, 1 - y]
+            ).astype(jnp.bfloat16)
+            y_copy(index, piece).start()
+            own[piece][block, y] = summed(
+                own[piece][block, y], from_core[piece][block, y]
+            ).astype(jnp.bfloat16)
+
+    def ring_pieces(flow, step):
+        return ((1,), (2, 0))[flow] if step == 0 else (0, 1, 2)
+
+    def ring_copy(flow, step, piece):
+        block = around(at.place, (-1 if flow else 1) * (4 - step))
+        return remote(
+            own[piece].at[block, y],
+            from_ring[piece].at[flow, step],
+            ring_s.at[flow, step, piece],
+            ring_r.at[flow, step, piece],
+            ring_device[flow],
+        )
+
+    def ring_step(step):
+        for flow in range(2):
+            block = around(at.place, (-1 if flow else 1) * (4 - step))
+            offset = (-1 if flow else 1) * (4 - step)
+            index = BLOCK_ORDER.index(4 if step == 0 else offset)
+            for piece in ring_pieces(flow, step):
+                y_copy(index, piece).wait_recv()
+                terms = [own[piece][block, y], from_y[piece][block]]
+                if step > 0 and piece in ring_pieces(flow, step - 1):
+                    ring_copy(flow, step - 1, piece).wait_recv()
+                    terms.append(from_ring[piece][flow, step - 1])
+                own[piece][block, y] = summed(*terms).astype(jnp.bfloat16)
+                ring_copy(flow, step, piece).start()
+
+    for copy in grads:
+        copy.wait_recv()
+    for seg in range(16):
+        slot = place_ref[seg]
+        do_tree[seg * 128 : seg * 128 + 128, :] = do_slots.reshape(16, 128, 128)[slot]
+    for block in range(8):
+        rows = pl.ds(block * 256, 256)
+        key_t[:, block * 256 : block * 256 + 256] = qkv_ref[rows, 128:256].T
+    dk[...] = jnp.zeros_like(dk)
+    dv[...] = jnp.zeros_like(dv)
+
+    for block in range(8):
+        masks = tile_masks(block, parents_ref)
+        rows = pl.ds(block * 256, 256)
+        across = pl.ds(block * 256, 256)
+
+        def one_head(head, unused):
+            head_rows = pl.ds(pl.multiple_of(head * HEAD, HEAD), HEAD)
+            queries = head_lanes(qkv_ref[rows, 0:128], head) * jnp.bfloat16(0.125)
+            grad_rows = head_lanes(do_tree[rows, :], head)
+            lse = log_ref[pl.ds(pl.multiple_of(head * 8, 8), 8), across][0:1]
+            grad_t = do_tree[rows, :].T.astype(jnp.float32)
+            both = grad_t * mixed_ref[:, across]
+            delta0 = jnp.sum(both[:HEAD], axis=0, keepdims=True)
+            delta1 = jnp.sum(both[HEAD:], axis=0, keepdims=True)
+            delta = jnp.where(head == 0, delta0, delta1)
+            grad_query = None
+            for first, count, scores in score_parts(
+                block, qkv_ref.at[:, pl.ds(128, 128)], queries, masks
+            ):
+                keys = pl.ds(first, count)
+                weights = jnp.exp(scores - lse)
+                grad_weights = times_t(qkv_ref[keys, 256:384], grad_rows)
+                grad_scores = (weights * (grad_weights - delta)).astype(jnp.bfloat16)
+                dk[keys, :] += jnp.dot(grad_scores, queries, preferred_element_type=jnp.float32)
+                dv[keys, :] += jnp.dot(
+                    weights.astype(jnp.bfloat16), grad_rows, preferred_element_type=jnp.float32
+                )
+                term = jnp.dot(
+                    key_t[head_rows, keys], grad_scores, preferred_element_type=jnp.float32
+                )
+                grad_query = term if grad_query is None else grad_query + term
+            dq_t[head_rows, across] = grad_query * 0.125
+            return unused
+
+        lax.fori_loop(0, 2, one_head, 0)
+        if block == 4:
+            ring_step(0)
+
+    for seg in range(16):
+        rows = pl.ds(seg * 128, 128)
+        gq_tree[seg, :, 0:128] = dq_t[:, seg * 128 : seg * 128 + 128].T.astype(jnp.bfloat16)
+        gq_tree[seg, :, 128:256] = dk[rows, :].astype(jnp.bfloat16)
+        gq_tree[seg, :, 256:384] = dv[rows, :].astype(jnp.bfloat16)
+    for slot in range(16):
+        gq_slots[slot // 2, (slot % 2) * 128 : (slot % 2) * 128 + 128, :] = gq_tree[ids_ref[slot]]
+
+    def ge_copy(flow, step):
+        source, target = cr_down.at[flow * 4 + step], ge_recv.at[flow, step]
+        if step == 0:
+            source, target = source.at[flow], target.at[flow]
+        return remote(
+            source, target, ge_s.at[flow, step], ge_r.at[flow, step], ring_device[flow]
+        )
+
+    def ge_part(block):
+        weights = slice_ref[...].reshape(1024, 384)
+        return times_t(gq_slots[block], weights)
+
+    def ge_step(step):
+        for flow in range(2):
+            block = around(at.place, (-1 if flow else 1) * (4 - step))
+            part = ge_part(block)
+            if step > 0:
+                ge_copy(flow, step - 1).wait_recv()
+            for half in range(2):
+                if step == 0 and half != flow:
+                    continue
+                rows = part[half * 128 : half * 128 + 128]
+                if step > 1 or (step == 1 and half == flow):
+                    rows = rows + ge_recv[flow, step - 1, half].astype(jnp.float32)
+                cr_down[flow * 4 + step, half] = rows.astype(jnp.bfloat16)
+            ge_copy(flow, step).start()
+
+    ge_step(0)
+    for block in range(8):
+        gq_t[:, block * 256 : block * 256 + 256] = gq_slots[block].T
+
+    slices = []
+    for step in range(1, 8):
+        to = at.other(step)
+        slices.append(
+            remote(qs_send.at[to], qs_recv.at[me], qs_s.at[step], qs_r.at[step], (rep, to))
+        )
+    for step in range(8):
+        to = at.other(step)
+        entered = ent_ref[:, :, pl.ds(pl.multiple_of(to * 128, 128), 128)].reshape(2048, 128)
+        made = jnp.dot(gq_t[...], entered, preferred_element_type=jnp.float32)
+        made = made.T.astype(jnp.bfloat16).reshape(2, 2, 32, 384)
+        if step == 0:
+            qs_recv[me] = made
+        else:
+            qs_send[to] = made
+            slices[step - 1].start()
+    ge_step(1)
+    ring_step(1)
+    for copy in slices:
+        copy.wait_recv()
+    qs_over_core = remote(
+        qs_recv.at[:, :, 1 - core], qs_core, qr_s.at[0], qr_r.at[0], (at.rep_core, me)
+    )
+    qs_over_core.start()
+    ge_step(2)
+    qs_over_core.wait_recv()
+    qs_half[...] = summed(qs_recv[:, :, core], qs_core[...]).astype(jnp.bfloat16)
+    qs_over_y = remote(qs_half.at[:, 1 - y], qs_y, qr_s.at[1], qr_r.at[1], (at.rep_y, me))
+    qs_over_y.start()
+    ring_step(2)
+    qs_over_y.wait_recv()
+    qkv_out[:, rep] = summed(qs_half[:, y], qs_y[...]).astype(jnp.bfloat16)
+    back_y = remote(
+        qkv_out.at[:, rep], qkv_out.at[:, rep], qr_s.at[2], qr_r.at[2], (at.rep_y, me)
+    )
+    back_core = remote(
+        qkv_out.at[:, rep], qkv_out.at[:, rep], qr_s.at[3], qr_r.at[3], (at.rep_core, me)
+    )
+    back_y.start()
+    back_core.start()
+    ge_step(3)
+    ring_step(3)
+    back_y.wait_recv()
+    back_far = remote(
+        qkv_out.at[:, at.rep_y], qkv_out.at[:, at.rep_y], qr_s.at[4], qr_r.at[4], (at.rep_core, me)
+    )
+    back_far.start()
+
+    for flow in range(2):
+        ge_copy(flow, 3).wait_recv()
+    grad_entered = ge_part(me)
+    for flow in range(2):
+        grad_entered = grad_entered + ge_recv[flow, 3].reshape(256, 1024).astype(jnp.float32)
+    normed, inv_std = normed_rows(tok_ref[...].astype(jnp.float32))
+    gain_sum = jnp.sum(grad_entered * normed, axis=0, keepdims=True)
+    in_ref[...] = gh_ref[...] + norm_back(grad_entered * gain_row(gains_ref, 0), normed, inv_std)
+    for s in range(8):
+        gp[s, 0:8, :] = jnp.broadcast_to(gain_sum[:, s * 128 : s * 128 + 128], (8, 128))
+        gp[s, 8:16, :] = jnp.broadcast_to(gfg_ref[:, s * 128 : s * 128 + 128], (8, 128))
+    gain_sends = []
+    for step in range(1, 8):
+        to = at.other(step)
+        gain_sends.append(
+            remote(gp.at[to], gp_recv.at[me], gp_s.at[step], gp_r.at[step], (rep, to))
+        )
+    for copy in gain_sends:
+        copy.start()
+    gp_recv[me] = gp[me]
+
+    def final_copy(piece, leg):
+        quarter = at.rep_y if leg == 2 else rep
+        rows = 32 if piece < 2 else 128
+        spot = result[piece].at[pl.ds(quarter * rows, rows), :]
+        device = (at.rep_y if leg == 0 else at.rep_core, me)
+        return remote(spot, spot, fin_s.at[piece, leg], fin_r.at[piece, leg], device)
+
+    for piece in range(3):
+        y_copy(7, piece).wait_recv()
+        terms = [own[piece][me, y], from_y[piece][me]]
+        for flow in range(2):
+            ring_copy(flow, 3, piece).wait_recv()
+            terms.append(from_ring[piece][flow, 3])
+        rows = 32 if piece < 2 else 128
+        result[piece][pl.ds(rep * rows, rows), :] = summed(*terms).astype(jnp.bfloat16)
+        final_copy(piece, 0).start()
+        final_copy(piece, 1).start()
+    for copy in gain_sends:
+        copy.wait_recv()
+    total = gp_recv[0]
+    for s in range(1, 8):
+        total = total + gp_recv[s]
+    gp_rep[rep] = total
+    rep_sends = [
+        remote(gp_rep.at[rep], gp_rep.at[rep], gr_s.at[i], gr_r.at[i], (to, me))
+        for i, to in enumerate((at.rep_y, at.rep_core, at.rep_far))
+    ]
+    for copy in rep_sends:
+        copy.start()
+    for piece in range(3):
+        final_copy(piece, 0).wait_recv()
+        final_copy(piece, 2).start()
+    for copy in rep_sends:
+        copy.wait()
+    gain_out[...] = gp_rep[0] + gp_rep[1] + gp_rep[2] + gp_rep[3]
+    for piece in range(3):
+        final_copy(piece, 1).wait()
+        final_copy(piece, 2).wait()
+        final_copy(piece, 0).wait_send()
+    back_core.wait()
+    back_far.wait()
+    back_y.wait_send()
+    qs_over_y.wait_send()
+    qs_over_core.wait_send()
+    for copy in slices + gain_sends + grads:
+        copy.wait_send()
+    for index in range(8):
+        for piece in range(3):
+            core_copy(index, piece).wait_send()
+            y_copy(index, piece).wait_send()
+    for step in range(4):
+        for flow in range(2):
+            ge_copy(flow, step).wait_send()
+            for piece in ring_pieces(flow, step):
+                ring_copy(flow, step, piece).wait_send()
+
+
+def backward_part(
+    places, slot_ids, parents, tokens, grad_hidden, grad_attn, entered, qkv, mixed, logs, gains,
+    slices, grad_gain_ffn, grad_out, grad_up, grad_down,
+):
+    smem = pl.BlockSpec(memory_space=pltpu.SMEM)
+    vmem = pl.BlockSpec(memory_space=pltpu.VMEM)
+    anywhere = pl.BlockSpec(memory_space=pl.ANY)
+    dma = pltpu.SemaphoreType.DMA
+    low, full = jnp.bfloat16, jnp.float32
+
+    def pieces(*lead):
+        return [
+            pltpu.VMEM(lead + (32, 1024), low),
+            pltpu.VMEM(lead + (32, 4096), low),
+            pltpu.VMEM(lead + (128, 1024), low),
+        ]
+
+    in_grad, qkv_part, out_part, up_part, down_part, gain_part = pl.pallas_call(
+        backward_kernel,
+        out_shape=[
+            jax.ShapeDtypeStruct((256, 1024), full),
+            jax.ShapeDtypeStruct((8, 4, 32, 384), low),
+            jax.ShapeDtypeStruct((128, 1024), low),
+            jax.ShapeDtypeStruct((128, 4096), low),
+            jax.ShapeDtypeStruct((512, 1024), low),
+            jax.ShapeDtypeStruct((16, 128), full),
+        ],
+        in_specs=[smem] * 3 + [vmem] * 10 + [anywhere] * 3,
+        out_specs=[vmem] * 6,
+        scratch_shapes=pieces(8, 2) + pieces(8, 2) + pieces(8) + pieces(2, 4) + [
+            pltpu.VMEM((8, 256, 128), low),
+            pltpu.VMEM((2048, 128), low),
+            pltpu.VMEM((128, 2048), low),
+            pltpu.VMEM((128, 2048), full),
+            pltpu.VMEM((2048, 128), full),
+            pltpu.VMEM((2048, 128), full),
+            pltpu.VMEM((16, 128, 384), low),
+            pltpu.VMEM((8, 256, 384), low),
+            pltpu.VMEM((384, 2048), low),
+            pltpu.VMEM((2, 4, 2, 128, 1024), low),
+            pltpu.VMEM((8, 2, 2, 32, 384), low),
+            pltpu.VMEM((8, 2, 2, 32, 384), low),
+            pltpu.VMEM((8, 2, 32, 384), low),
+            pltpu.VMEM((8, 2, 32, 384), low),
+            pltpu.VMEM((8, 32, 384), low),
+            pltpu.VMEM((8, 16, 128), full),
+            pltpu.VMEM((8, 16, 128), full),
+            pltpu.VMEM((4, 16, 128), full),
+            dma((8,)), dma((8,)), dma((3,)), dma((8, 3)), dma((8, 3)), dma((8, 3)), dma((8, 3)),
+            dma((2, 4, 3)), dma((2, 4, 3)), dma((3, 3)), dma((3, 3)), dma((2, 4)), dma((2, 4)),
+            dma((8,)), dma((8,)), dma((5,)), dma((5,)), dma((8,)), dma((8,)), dma((3,)), dma((3,)),
+        ],
+        compiler_params=pltpu.CompilerParams(
+            collective_id=2, has_side_effects=True, vmem_limit_bytes=62 * 2**20
+        ),
+    )(
+        places, slot_ids, parents, tokens, grad_hidden, grad_attn, entered, qkv, mixed, logs, gains,
+        slices, grad_gain_ffn.reshape(1, 1024), grad_out.reshape(8, 2, 2, 32, 1024),
+        grad_up.reshape(8, 2, 2, 32, 4096), grad_down.reshape(8, 2, 2, 128, 1024),
+    )
+    qkv_part = qkv_part.reshape(8, 128, 3, 128).transpose(1, 2, 0, 3).reshape(128, 3072)
+    return (in_grad, qkv_part, out_part, up_part, down_part, gain_part)
+
+
+def fast_shards(
+    tokens, cotangent, qkv_weight, out_weight, up_weight, down_weight, gain_attn, gain_ffn, parents, slot_ids
+):
+    seg_range = jnp.arange(16, dtype=jnp.int32)
+    places = jnp.sum(
+        jnp.where(slot_ids[None, :] == seg_range[:, None], seg_range[None, :], 0), axis=1
+    )
+    parents = parents.reshape(16)
+    wq = qkv_weight.astype(jnp.bfloat16).reshape(128, 3, 8, 128).transpose(2, 0, 1, 3)
+    wq = wq.reshape(8, 128, 384)
+    out_b = out_weight.astype(jnp.bfloat16)
+    up_b = up_weight.astype(jnp.bfloat16)
+    down_b = down_weight.astype(jnp.bfloat16)
+    gains = jnp.concatenate(
+        [jnp.broadcast_to(g.astype(jnp.bfloat16)[None], (8, 128)) for g in (gain_attn, gain_ffn)]
+    )
+    attended, entered, qkv, mixed, logs, gains, slices, out_full, up_full, down_full = forward_part(
+        places, slot_ids, parents, tokens, wq, gains, out_b, up_b, down_b
+    )
+    attn_gain = gains[:, 0, :].reshape(1, 1024).astype(jnp.float32)
+    ffn_gain = gains[:, 8, :].reshape(1, 1024).astype(jnp.float32)
+    hidden = tokens.astype(jnp.float32) + jnp.dot(
+        attended, out_full, preferred_element_type=jnp.float32
+    )
+    normed_two, inv_two = normalize(hidden)
+    second = (normed_two * ffn_gain).astype(jnp.bfloat16)
+    pre_act = jnp.dot(second, up_full, preferred_element_type=jnp.float32)
+    active = gelu_exact(pre_act).astype(jnp.bfloat16)
+    output = (hidden + jnp.dot(active, down_full, preferred_element_type=jnp.float32)).astype(
+        jnp.bfloat16
+    )
+    grad_down = t_times(active, cotangent).astype(jnp.bfloat16)
+    grad_active = times_t(cotangent, down_full).astype(jnp.bfloat16)
+    grad_pre = (grad_active.astype(jnp.float32) * gelu_slope(pre_act)).astype(jnp.bfloat16)
+    grad_up = t_times(second, grad_pre).astype(jnp.bfloat16)
+    grad_second = times_t(grad_pre, up_full)
+    grad_gain_ffn = jnp.sum(grad_second * normed_two, axis=0)
+    grad_hidden = cotangent.astype(jnp.float32) + norm_back(
+        grad_second * ffn_gain, normed_two, inv_two
+    )
+    grad_y = grad_hidden.astype(jnp.bfloat16)
+    grad_out = t_times(attended, grad_y).astype(jnp.bfloat16)
+    grad_attn = times_t(grad_y, out_full).astype(jnp.bfloat16)
+    input_grad, qkv_part, out_part, up_part, down_part, gain_part = backward_part(
+        places, slot_ids, parents, tokens, grad_hidden, grad_attn, entered, qkv, mixed, logs, gains,
+        slices, grad_gain_ffn, grad_out, grad_up, grad_down,
+    )
+    return (
+        output,
+        input_grad,
+        qkv_part.astype(jnp.float32),
+        out_part.astype(jnp.float32),
+        up_part.astype(jnp.float32),
+        down_part.astype(jnp.float32),
+        gain_part[0],
+        gain_part[8],
+    )
 
 
 def solution(mesh):
@@ -346,4 +1162,17 @@
         P("shard"),
         P("shard"),
     )
-    return jax.shard_map(shards, mesh=mesh, in_specs=in_specs, out_specs=out_specs, check_vma=False)
+
+    def fits(*args):
+        shapes = [a.shape for a in args]
+        return shapes[0] == (8192, 1024) and shapes[4] == (1024, 4096) and shapes[8] == (4, 16)
+
+    small = mesh.shape["rep"] == 4 and mesh.shape["shard"] == 8
+
+    def whole(*args):
+        run = fast_shards if small and fits(*args) else shards
+        return jax.shard_map(
+            run, mesh=mesh, in_specs=in_specs, out_specs=out_specs, check_vma=False
+        )(*args)
+
+    return whole

time: 1910 us -> 370 us (0.19)
  waiting for transfers between devices: 1530 us -> 0 us
  Pallas kernels: 0 us -> 299 us
  matrix products: 152 us -> 32.9 us
  blocking collectives: 65.5 us -> 0 us
  local copies, waits for them, and re-layouts: 69.3 us -> 12.8 us
  other arithmetic: 60.3 us -> 17.9 us
    reduce_scatter x5 -> x0, waiting for transfers between devices: 1110 us -> none  [the longest x1 284 us: shards(): lax.psum_scatter(grad_up, 'shard', scatter_dimension=0, tiled=True)]
    all_gather x6 -> x0, waiting for transfers between devices: 393 us -> none  [the longest x1 117 us: shards(): lax.all_gather(down_weight.astype(jnp.bfloat16), 'shard', axis=0, tiled=T...]
    pallas_call x0 -> x2, Pallas kernels: none -> 299 us  [the longest x1 162 us: backward_part(): pl.pallas_call(backward_kernel, out_shape=[jax.ShapeDtypeStruct((256, 102...]
    dot_general x50 -> x3, matrix products: 105 us -> 11.1 us  [the longest x1 5.37 us: fast_shards(): pre_act = jnp.dot(second, up_full, preferred_element_type=jnp.float32)]
    all_gather x2 -> x0, blocking collectives: 40.1 us -> none  [the longest x1 22.3 us: shards(): lax.all_gather(gain_attn.astype(jnp.bfloat16), 'shard', axis=0, tiled=True)]
    psum x1 -> x0, waiting for transfers between devices: 28.5 us -> none  [shards(): lax.psum(group_sums[0].astype(jnp.bfloat16), 'rep').astype(jnp.float32)]
    reshape x2 -> x1, local copies, waits for them, and re-layouts: 23.5 us -> 1.17 us  [fast_shards(): wq = wq.reshape(8, 128, 384)]
    unnamed x1 -> x0, blocking collectives: 19.8 us -> none
  transfers between devices with their start and end apart: 12 -> 0, of which waited for: 11 -> 0; matrix products, arithmetic and copies ran while one was open for 9% -> 0% of each run, Pallas kernels for 0% -> 0%
where the time goes in v1:
time: 370 us; the launch traced here: 364 us
  Pallas kernels  299 us (81%)
  matrix products  32.9 us (9%)
  other arithmetic  17.9 us (5%)
  local copies, waits for them, and re-layouts  12.8 us (3%)
    pallas_call x1, Pallas kernels, backward_part(): pl.pallas_call(backward_kernel, out_shape=[jax.ShapeDtypeStruct((256, 102...  162 us
    pallas_call x1, Pallas kernels, forward_part(): pl.pallas_call(forward_kernel, out_shape=[jax.ShapeDtypeStruct((256, 1024...  137 us
    dot_general x3, matrix products, t_times(): lax.dot_general(left_side, right_side, (((0,), (0,)), ((), ())), preferre...  13.4 us
    dot_general x3, matrix products, times_t(): lax.dot_general(left_side, right_side, (((1,), (1,)), ((), ())), preferre...  8.37 us

profile of v1, /device:TPU:0, one launch (start us, length us, event | category | flops | bytes accessed | tf_op | source)
XLA Modules:
  0.0 363.5 jit_solution(9876956815940644709)
XLA Ops:
  0.6 1.3 select_reduce_fusion.place_ref
  1.9 0.7 convert_element_type.95
  2.6 0.7 convert_element_type.96
  3.2 0.6 pad_maximum_fusion.gain_ref
  3.8 1.8 convert_element_type.97.out_ref
  5.6 1.8 copy.29
  7.5 1.2 copy.31.wq_ref
  8.6 2.7 convert_element_type.98.up_ref
  11.3 2.8 convert_element_type.99.down_ref
  14.1 136.8 %shard_map.161 = (bf16[256,1024]{1,0:T(8,128)(2,1)}, bf16[8,256,1024]{2,1,0:T(8,128)(2,1)}, bf16[2048,384]{1,0:T(8,128)(2,1)}, f32[128,2048]{1,0:T(8,128)}, f32[...) custom-call(s32[16]{0:T(128)} %select_reduce_fusion.place_ref, ...), custom_call_target="tpu_custom_call" | custom-call | tf_op jit(solution)/shard_map/pallas_call | solution.py:656
  150.9 0.7 slice_convert_fusion
  151.6 2.6 fusion.12
  154.2 0.2 multiply_reduce_fusion.2
  154.5 5.4 %multiply_convert_fusion = (bf16[256,4096]{1,0:T(8,128)(2,1)S(1)}, f32[256,4096]{1,0:T(8,128)S(1)}) fusion(bf16[1024,4096]{1,0:T(8,128)(2,1)} %get-tuple-element.27, f32[256,1024]{1,0:T(8,128)S(1)} %get-tuple-element.62, f32[1024]{0:T(1024)S(1)} %bitcast.45, f32[256]{0:T(256)S(1)} %add_rsqrt_fusion, f32[256]{0:T(256)S(1)} %broadcast_multiply_fusion.2), kind=kOutput, calls=%fused_computation.12 | convolution fusion | flops 2153775104 | bytes 15734784 | tf_op jit(solution)/shard_map/dot_general | solution.py:1109
  159.9 0.4 slice-done.3
  160.3 3.6 %fusion.3 = bf16[256,4096]{1,0:T(8,128)(2,1)S(1)} fusion(bf16[4096,1024]{1,0:T(8,128)(2,1)S(1)} %bitcast.55, bf16[256,1024]{1,0:T(8,128)(2,1)S(1)} %copy-done.3, f32[256,4096]{1,0:T(8,128)S(1)} %get-tuple-element.64), kind=kOutput, calls=%fused_computation.7 | convolution fusion | flops 2160066560 | bytes 15204352 | tf_op jit(solution)/shard_map/dot_general | solution.py:45
  164.0 3.1 fusion.8
  167.1 3.2 multiply_reduce_fusion
  170.3 0.4 multiply_add_fusion.gh_ref
  170.7 1.6 convolution_convert_fusion.4.ga_ref
  172.3 2.1 convolution_convert_fusion.3
  174.4 5.7 %convolution_convert_fusion.1 = bf16[1024,4096]{1,0:T(8,128)(2,1)} fusion(bf16[256,4096]{1,0:T(8,128)(2,1)S(1)} %fusion.3, f32[256,1024]{1,0:T(8,128)S(1)} %get-tuple-element.62, f32[1024]{0:T(1024)S(1)} %bitcast.48, f32[256]{0:T(256)S(1)} %add_rsqrt_fusion, f32[256]{0:T(256)S(1)} %broadcast_multiply_fusion.2), kind=kOutput, calls=%fused_computation.1 | convolution fusion | flops 2152726528 | bytes 11540480 | tf_op jit(solution)/shard_map/dot_general | solution.py:51
  180.1 5.6 %convolution_convert_fusion = bf16[4096,1024]{1,0:T(8,128)(2,1)} fusion(bf16[256,4096]{1,0:T(8,128)(2,1)S(1)} %get-tuple-element.63, bf16[256,1024]{1,0:T(8,128)(2,1)S(1)} %copy-done.3), kind=kOutput, calls=%fused_computation | convolution fusion | flops 2151677952 | bytes 11010048 | tf_op jit(solution)/shard_map/dot_general | solution.py:51
  185.7 161.9 %shard_map.162 = (f32[256,1024]{1,0:T(8,128)}, bf16[8,4,32,384]{3,2,1,0:T(8,128)(2,1)}, bf16[128,1024]{1,0:T(8,128)(2,1)}, bf16[128,4096]{1,0:T(8,128)(2,1)}, bf...) custom-call(s32[16]{0:T(128)} %select_reduce_fusion.place_ref, s32[16]{0:T(128)} %ids_ref.3, s32[16]{0:T(128)} %bitcast.51, ...), custom_call_target="tpu_custom_call" | custom-call | tf_op jit(solution)/shard_map/pallas_call | solution.py:1036
  347.7 1.2 slice_bitcast_fusion
  348.9 1.8 convert_element_type.119
  350.7 2.4 reshape.84
  353.1 1.6 copy.33
  354.7 3.1 copy.34
  357.8 2.8 convert_element_type.120
  360.5 1.6 convert_element_type.121
  362.1 1.0 copy.37
  (29 shorter events, 0.1 us)
Async XLA Ops:
  11.3 140.3 %copy-start.2 = (bf16[256,1024]{1,0:T(8,128)(2,1)S(1)}, bf16[256,1024]{1,0:T(8,128)(2,1)}, u32[]{:S(2)}) copy-start(bf16[256,1024]{1,0:T(8,128)(2,1)} %tok_ref.3) | copy-start | bytes 1572868
  154.2 5.7 %slice-start.2 = ((s8[8388608]{0:T(1024)(128)(4,1)}), s8[4194304]{0:T(1024)(128)(4,1)S(1)}, s32[]{:S(2)}) async-start(s8[8388608]{0:T(1024)(128)(4,1)} %bitcast.54), calls=%async_computation.2 | async-start | bytes 8388608
  154.5 5.4 %copy-start.3 = (bf16[256,1024]{1,0:T(8,128)(2,1)S(1)}, bf16[256,1024]{1,0:T(8,128)(2,1)}, u32[]{:S(2)}) copy-start(bf16[256,1024]{1,0:T(8,128)(2,1)} %param.11) | copy-start | bytes 1572868
  154.5 5.9 %slice-start.3 = ((s8[8388608]{0:T(1024)(128)(4,1)}), s8[4194304]{0:T(1024)(128)(4,1)S(1)}, s32[]{:S(2)}) async-start(s8[8388608]{0:T(1024)(128)(4,1)} %bitcast.54), calls=%async_computation.3 | async-start | bytes 8388608
  154.5 12.6 %slice-start = ((s8[8388608]{0:T(1024)(128)(4,1)}), s8[4194304]{0:T(1024)(128)(4,1)S(1)}, s32[]{:S(2)}) async-start(s8[8388608]{0:T(1024)(128)(4,1)} %bitcast.52), calls=%async_computation | async-start | bytes 8388608
  160.3 6.8 %slice-start.1 = ((s8[8388608]{0:T(1024)(128)(4,1)}), s8[4194304]{0:T(1024)(128)(4,1)S(1)}, s32[]{:S(2)}) async-start(s8[8388608]{0:T(1024)(128)(4,1)} %bitcast.52), calls=%async_computation.1 | async-start | bytes 8388608
  167.1 3.6 copy-start.1
  170.3 2.0 copy-start.4
  170.7 9.4 %copy-start = (f32[256,1024]{1,0:T(8,128)}, f32[256,1024]{1,0:T(8,128)S(1)}, u32[]{:S(2)}) copy-start(f32[256,1024]{1,0:T(8,128)S(1)} %multiply_add_fusion.gh_ref) | copy-start | bytes 3145732
  353.1 7.5 %copy-start.5 = (bf16[512,1024]{1,0:T(8,128)(2,1)S(1)}, bf16[512,1024]{1,0:T(8,128)(2,1)}, u32[]{:S(2)}) copy-start(bf16[512,1024]{1,0:T(8,128)(2,1)} %get-tuple-element.38) | copy-start | bytes 3145732
  354.7 7.4 %copy-start.6 = (f32[256,1024]{1,0:T(8,128)S(1)}, f32[256,1024]{1,0:T(8,128)}, u32[]{:S(2)}) copy-start(f32[256,1024]{1,0:T(8,128)} %get-tuple-element.77) | copy-start | bytes 3145732
